TPU v7x, 512 devices: a whole 4x8x8 slice. The times are simulated.
512 devices in a mesh: occ: 16 (over y, core), vir: 32 (over x, z).
Axes of the slice: x: 4, y: 8, z: 8, core: 2. Of those that a mesh axis runs over, the one named last changes fastest.
Arguments:
- amplitudes: float32 [2048, 12288], P('occ', 'vir'), may hold values from -6 to 6
- integrals: float32 [12288, 4096], P('vir', 'occ'), may hold values from -0.109375 to 0.109375
- pair_mask: int32 [32, 192], P('occ', 'vir'), may hold values 0 or 1
- tile_mask: int32 [192, 64], P('vir', 'occ'), may hold values 0 or 1
Outputs:
- residual: float32 [2048, 4096], P('occ', 'vir')
Inputs may be any that keep to these rules, and one draw needn't show every extreme that they name: `pair_mask`: 0 marks a tile that is absent and contributes nothing. `tile_mask`: 0 marks a tile that is absent and contributes nothing.
All inputs are finite; a program needn't handle non-finite values. No bound on the sum of `pair_mask` or of `tile_mask` on one device may be relied on, other than what follows from the above.
Results may differ from a plain program's by a relative error of at most 0.00007.
Values sent between devices are 32-bit elements; how exact they have to be, the bound alone decides.
No kernel may reach another device: no remote copies, remote signals or barrier semaphores. Data moves between devices by JAX's collectives and lax.ppermute only.
A program may use at most 64 MiB of HBM per device.

v0:
```python
import jax
import jax.numpy as jnp
from jax import lax
from jax.sharding import PartitionSpec as P


def expand(mask, width):
    grown = jnp.repeat(mask.astype(jnp.float32), width, axis=0)
    return jnp.repeat(grown, width, axis=1)


def body(amplitudes, integrals, pair_mask, tile_mask):
    tile_width = amplitudes.shape[1] // pair_mask.shape[1]
    masked_t = amplitudes * expand(pair_mask, tile_width)
    masked_v = integrals * expand(tile_mask, tile_width)
    partial_sum = jnp.dot(
        masked_t,
        lax.all_gather(masked_v, "occ", axis=1, tiled=True),
        precision=lax.Precision.HIGHEST,
        preferred_element_type=jnp.float32,
    )
    return lax.psum_scatter(partial_sum, "vir", scatter_dimension=1, tiled=True)


def solution(mesh):
    in_specs = (P("occ", "vir"), P("vir", "occ"), P("occ", "vir"), P("vir", "occ"))
    out_specs = P("occ", "vir")
    return jax.shard_map(body, mesh=mesh, in_specs=in_specs, out_specs=out_specs, check_vma=False)
```

profile of v0, /device:TPU:8, one launch (start us, length us, event | category | flops | bytes accessed | tf_op | source)
XLA Modules:
  0.0 302.7 jit_solution(3729471157549326904)
XLA Ops:
  6.5 0.0 all-gather.2.cloned.1.call-start
  6.5 0.7 convert_element_type.7
  7.2 0.1 broadcast_in_dim.14
  7.3 0.1 reshape.14
  7.4 1.2 copy.11
  8.5 0.8 bitcast_multiply_fusion
  9.3 0.0 all-gather.2.cloned.1.call-update
  9.3 0.0 reduce-scatter.2.cloned.1.call-start
  9.4 0.7 convert_element_type.6
  10.1 0.1 copy.9
  10.2 0.1 broadcast_in_dim.12
  10.2 0.1 reshape.12
  10.3 1.1 copy.10
  11.4 51.0 %all-gather.2.cloned.1.call-done = f32[384,4096]{0,1:T(8,128)} async-done(((f32[384,256]{0,1:T(8,128)}), f32[384,4096]{0,1:T(8,128)}) %all-gather.2.cloned.1.call-update) | async-done | bytes 6291472 | tf_op jit(solution)/shard_map/all_gather | solution.py:18
  62.4 10.7 %fusion = f32[128,4096]{1,0:T(8,128)} fusion(f32[128,384]{0,1:T(8,128)S(1)} %bitcast_multiply_fusion.1, f32[384,4096]{0,1:T(8,128)} %all-gather.2.cloned.1.call-done), kind=kOutput, calls=%fused_computation.2 | convolution fusion | flops 2415919104 | bytes 8585216 | tf_op jit(solution)/shard_map/dot_general | solution.py:16
  73.0 0.0 reduce-scatter.2.cloned.1.call-update
  73.1 222.8 %reduce-scatter.2.cloned.1.call-done = f32[128,128]{1,0:T(8,128)} async-done(((f32[128,4096]{1,0:T(8,128)}), f32[128,128]{1,0:T(8,128)}) %reduce-scatter.2.cloned.1.call-update) | async-done | bytes 65552 | tf_op jit(solution)/shard_map/reduce_scatter | solution.py:22
  (1 shorter events, 0.0 us)
Async XLA Ops:
  6.5 55.9 %all-gather.2.cloned.1.call-start = ((), (), s32[]{:S(2)}) async-start(), calls=%async_computation.1 | async-start | bytes 6684672 | tf_op jit(solution)/shard_map/all_gather | solution.py:18
  9.3 286.5 %reduce-scatter.2.cloned.1.call-start = ((), (), s32[]{:S(2)}) async-start(), calls=%async_computation.2 | async-start | bytes 2162688 | tf_op jit(solution)/shard_map/reduce_scatter | solution.py:22
Sparse Core Ops, SparseCore 0:
  9.5 52.8 all-gather.1
  73.2 222.6 reduce-scatter.1
where the time goes:
time: 303 us
  waiting for transfers between devices  274 us (90%)
  between operations  13.4 us (4%)
  matrix products  10.7 us (4%)
    reduce_scatter x1, waiting for transfers between devices, body(): return lax.psum_scatter(partial_sum, 'vir', scatter_dimension=1, tiled=True)  223 us
    all_gather x1, waiting for transfers between devices, body(): lax.all_gather(masked_v, 'occ', axis=1, tiled=True)  51 us
    dot_general x1, matrix products, body(): jnp.dot(masked_t, lax.all_gather(masked_v, 'occ', axis=1, tiled=True), pr...  10.7 us
  transfers between devices with their start and end apart: 2, of which 2 were waited for; matrix products, arithmetic and copies ran while one was open for 1% of the time, Pallas kernels for 0%

commit v1 on v0

--- a/solution.py
+++ b/solution.py
@@ -15,7 +15,15 @@
     masked_v = integrals * expand(tile_mask, tile_width)
     partial_sum = jnp.dot(
         masked_t,
-        lax.all_gather(masked_v, "occ", axis=1, tiled=True),
+        jnp.concatenate(
+            lax.all_to_all(
+                jnp.stack([masked_v for _ in range(lax.axis_size("occ"))]),
+                "occ",
+                concat_axis=0,
+                split_axis=0,
+            ),
+            axis=1,
+        ),
         precision=lax.Precision.HIGHEST,
         preferred_element_type=jnp.float32,
     )

time: 303 us -> 402 us (1.33)
  waiting for transfers between devices: 274 us -> 362 us
  starting transfers between devices: 0.04 us -> 10.4 us
    all_to_all x0 -> x1, waiting for transfers between devices: none -> 137 us  [body(): lax.all_to_all(jnp.stack([masked_v for _ in range(lax.axis_size('occ'))])...]
    all_gather x1 -> x0, waiting for transfers between devices: 51 us -> none  [body(): lax.all_gather(masked_v, 'occ', axis=1, tiled=True)]
    all_to_all x0 -> x1, starting transfers between devices: none -> 10.3 us  [body(): lax.all_to_all(jnp.stack([masked_v for _ in range(lax.axis_size('occ'))])...]
  transfers between devices with their start and end apart: 2 -> 2, of which waited for: 2 -> 2; matrix products, arithmetic and copies ran while one was open for 1% -> 0% of each run, Pallas kernels for 0% -> 0%
where the time goes in v1:
time: 402 us
  waiting for transfers between devices  362 us (90%)
  between operations  13.5 us (3%)
  matrix products  10.6 us (3%)
  starting transfers between devices  10.4 us (3%)
  local copies, waits for them, and re-layouts  4.95 us (1%)
    reduce_scatter x1, waiting for transfers between devices, body(): return lax.psum_scatter(partial_sum, 'vir', scatter_dimension=1, tiled=True)  225 us
    all_to_all x1, waiting for transfers between devices, body(): lax.all_to_all(jnp.stack([masked_v for _ in range(lax.axis_size('occ'))])...  137 us
    dot_general x1, matrix products, body(): jnp.dot(masked_t, jnp.concatenate(lax.all_to_all(jnp.stack([masked_v for...  10.6 us
    all_to_all x1, starting transfers between devices, body(): lax.all_to_all(jnp.stack([masked_v for _ in range(lax.axis_size('occ'))])...  10.3 us
  transfers between devices with their start and end apart: 2, of which 2 were waited for; matrix products, arithmetic and copies ran while one was open for 0% of the time, Pallas kernels for 0%

profile of v1, /device:TPU:8, one launch (start us, length us, event | category | flops | bytes accessed | tf_op | source)
XLA Modules:
  0.0 401.9 jit_solution(9843134684687615133)
XLA Ops:
  6.5 1.2 copy.11
  7.7 0.7 convert_element_type.7
  8.4 0.1 broadcast_in_dim.14
  8.5 0.1 reshape.22
  8.6 3.3 stack.2
  11.8 0.0 copy-start
  11.8 0.0 copy-start.1
  11.8 10.3 %all-to-all-start = ((f32[16,384,256]{1,2,0:T(8,128)}), f32[16,384,256]{1,2,0:T(8,128)}, u32[]{:S(2)}, u32[]{:S(2)}) async-start(f32[16,384,256]{1,2,0:T(8,128)} %stack.2), calls=%async_computation | async-start | bytes 12582912 | tf_op jit(solution)/shard_map/all_to_all | solution.py:19
  22.2 0.0 reduce-scatter.2.cloned.1.call-start
  22.2 0.0 copy-done
  22.2 0.1 copy.10
  22.4 0.0 copy-done.1
  22.4 0.1 copy.9
  22.5 0.1 broadcast_in_dim.12
  22.5 0.1 reshape.20
  22.7 137.0 %all-to-all-done = f32[16,384,256]{1,2,0:T(8,128)} async-done(((f32[16,384,256]{1,2,0:T(8,128)}), f32[16,384,256]{1,2,0:T(8,128)}, u32[]{:S(2)}, u32[]{:S(2)}) %all-to-all-start) | async-done | bytes 6291488 | tf_op jit(solution)/shard_map/all_to_all | solution.py:19
  159.6 10.6 %fusion = f32[128,4096]{1,0:T(8,128)} fusion(f32[128,384]{0,1:T(8,128)S(1)} %bitcast_multiply_fusion.1, f32[384,4096]{0,1:T(8,128)} %bitcast.3), kind=kOutput, calls=%fused_computation.2 | convolution fusion | flops 2415919104 | bytes 8585216 | tf_op jit(solution)/shard_map/dot_general | solution.py:16
  170.3 0.0 reduce-scatter.2.cloned.1.call-update
  170.3 224.7 %reduce-scatter.2.cloned.1.call-done = f32[128,128]{1,0:T(8,128)} async-done(((f32[128,4096]{1,0:T(8,128)}), f32[128,128]{1,0:T(8,128)}) %reduce-scatter.2.cloned.1.call-update) | async-done | bytes 65552 | tf_op jit(solution)/shard_map/reduce_scatter | solution.py:30
  (3 shorter events, 0.1 us)
Async XLA Ops:
  11.8 10.4 %copy-start = (f32[128,384]{1,0:T(8,128)S(1)}, f32[128,384]{1,0:T(8,128)}, u32[]{:S(2)}) copy-start(f32[128,384]{1,0:T(8,128)} %param.4) | copy-start | bytes 589828
  11.8 10.5 %copy-start.1 = (s32[2,6]{1,0:T(2,128)S(1)}, s32[2,6]{1,0:T(2,128)}, u32[]{:S(2)}) copy-start(s32[2,6]{1,0:T(2,128)} %param.6) | copy-start | bytes 148
  11.8 147.8 %all-to-all-start = ((f32[16,384,256]{1,2,0:T(8,128)}), f32[16,384,256]{1,2,0:T(8,128)}, u32[]{:S(2)}, u32[]{:S(2)}) async-start(f32[16,384,256]{1,2,0:T(8,128)} %stack.2), calls=%async_computation | async-start | bytes 12582912 | tf_op jit(solution)/shard_map/all_to_all | solution.py:19
  22.2 372.9 %reduce-scatter.2.cloned.1.call-start = ((), (), s32[]{:S(2)}) async-start(), calls=%async_computation.2 | async-start | bytes 2162688 | tf_op jit(solution)/shard_map/reduce_scatter | solution.py:30
Sparse Core Ops, SparseCore 0:
  170.4 224.5 reduce-scatter.1
